TPU v7x, 32 devices: a whole 2x2x4 slice. The times are simulated.
32 devices in a mesh: blk: 8 (over z, y), team: 4 (over x, core).
Axes of the slice: x: 2, y: 2, z: 4, core: 2. Of those that a mesh axis runs over, the one named last changes fastest.
Arguments:
- loadings: bfloat16 [64, 98304], P(None, ('blk', 'team')), may hold values from -6 to 6
- scales: bfloat16 [64, 768], P(None, ('blk', 'team')), may hold values from 0.25 to 4
- cov: bfloat16 [2048, 2, 4, 12288], P('blk', None, 'team'), may hold values from -0.01953125 to 0.01953125
Outputs:
- product: float32 [64, 2048], P(None, 'blk')
All inputs are finite; a program needn't handle non-finite values.
Results may differ from a plain program's by a relative error of at most 0.0028.
Values may be sent and summed in bfloat16 or wider, within the bound.
A program may use at most 128 MiB of HBM per device.

v0:
```python
import jax
import jax.numpy as jnp
from jax import lax
from jax.sharding import PartitionSpec as P


def passed_along(x, axis, by):
    size = lax.axis_size(axis)
    return lax.ppermute(x, axis, [(i, (i + by) % size) for i in range(size)])


def per_device(loadings, scales, cov):
    team_size = lax.axis_size("team")
    cycle_size = lax.axis_size("blk")
    cycle_stops = cycle_size // team_size
    cycle_pos = lax.axis_index("blk")
    member = lax.axis_index("team")
    skew_lag = jnp.mod(cycle_pos - member, team_size)
    base_stop = jnp.mod((cycle_pos - skew_lag - member) // team_size, cycle_stops)
    held_block = (
        lax.all_gather(loadings, "team", axis=1, tiled=True),
        lax.all_gather(scales, "team", axis=1, tiled=True),
    )
    near_copy = passed_along((held_block[0], held_block[1]), "blk", 1)
    far_copies = passed_along((held_block[0], held_block[1], near_copy[0], near_copy[1]), "blk", 2)
    stacked_loads = jnp.stack([held_block[0], near_copy[0], far_copies[0], far_copies[2]])
    stacked_scales = jnp.stack([held_block[1], near_copy[1], far_copies[1], far_copies[3]])
    start_block = (
        lax.dynamic_index_in_dim(stacked_loads, skew_lag, 0, keepdims=False),
        lax.dynamic_index_in_dim(stacked_scales, skew_lag, 0, keepdims=False),
    )
    cov_local = cov[:, :, 0, :]
    n_loads = loadings.shape[0]
    row_count = cov.shape[0]

    def contribute(running, block, stop_num):
        block_load, block_scale = block
        groups = block_scale.shape[1]
        scaled = (
            (
                block_load.astype(jnp.float32).reshape(
                    n_loads, groups, block_load.shape[1] // groups
                )
                * block_scale.astype(jnp.float32)[:, :, None]
            )
            .reshape(n_loads, block_load.shape[1])
            .astype(jnp.bfloat16)
        )
        cov_slab = lax.dynamic_index_in_dim(
            cov_local, jnp.mod(stop_num, cycle_stops), 1, keepdims=False
        )
        term = lax.dot_general(
            scaled, cov_slab, (((1,), (1,)), ((), ())), preferred_element_type=jnp.float32
        )
        return running + term

    initial = jnp.zeros((n_loads, row_count), jnp.float32)
    running = contribute(initial, start_block, base_stop)

    def onward(stop_num, carry):
        partial_sum, moving = carry
        moving = passed_along((moving[0], moving[1]), "blk", team_size)
        return (contribute(partial_sum, moving, base_stop - stop_num), moving)

    running, _ = lax.fori_loop(1, cycle_stops, onward, (running, start_block))
    product = lax.psum(running, "team")
    return product


def solution(mesh):
    placed = (P(None, ("blk", "team")), P(None, ("blk", "team")), P("blk", None, "team", None))
    return jax.shard_map(
        per_device, mesh=mesh, in_specs=placed, out_specs=P(None, "blk"), check_vma=False
    )
```

profile of v0, /device:TPU:5, one launch (start us, length us, event | category | flops | bytes accessed | tf_op | source)
XLA Modules:
  0.0 257.0 jit_solution(3396251162267106322)
XLA Ops:
  6.5 0.0 all-gather.2.cloned.1.call-start
  6.5 0.7 all-gather.2.cloned.1.call-update
  7.3 0.0 all-reduce.2.cloned.1.call-start
  7.3 22.9 %all-gather.2.cloned.1.call-done = bf16[64,12288]{1,0:T(8,128)(2,1)} async-done(((bf16[64,3072]{1,0:T(8,128)(2,1)}), bf16[64,12288]{1,0:T(8,128)(2,1)}) %all-gather.2.cloned.1.call-update) | async-done | bytes 1572880 | tf_op jit(solution)/shard_map/all_gather | solution.py:21
  30.2 1.2 collective-permute-start
  31.4 1.2 collective-permute-start.1
  32.6 33.5 %collective-permute-done = bf16[64,12288]{1,0:T(8,128)(2,1)S(1)} collective-permute-done((bf16[64,12288]{1,0:T(8,128)(2,1)}, bf16[64,12288]{1,0:T(8,128)(2,1)S(1)}, u32[]{:S(2)}, u32[]{:S(2)}) %collective-permute-start) | collective-permute-done | bytes 1572896 | tf_op jit(solution)/shard_map/ppermute | solution.py:9
  66.1 1.2 collective-permute-start.2
  67.3 6.6 %all_gather.7 = bf16[64,96]{0,1:T(8,128)(2,1)S(1)} all-gather(bf16[64,24]{0,1:T(8,128)(2,1)} %param.4), channel_id=1, replica_groups=mesh['blk'=8,'team'=4] {'team'}, dimensions={1}, use_global_device_ids=true | all-gather | bytes 15360 | tf_op jit(solution)/shard_map/all_gather | solution.py:22
  73.9 0.1 copy.7
  74.0 2.8 %collective-permute-start.3 = (bf16[64,96]{1,0:T(8,128)(2,1)S(1)}, bf16[64,96]{1,0:T(8,128)(2,1)S(1)}, u32[]{:S(2)}, u32[]{:S(2)}) collective-permute-start(bf16[64,96]{1,0:T(8,128)(2,1)S(1)} %copy.7), channel_id=1, source_target_pairs={{0,4},{4,8},{8,12},{12,16},{16,20},{20,24},{24,28},{28,0},{1,5},{5... | collective-permute-start | bytes 36872 | tf_op jit(solution)/shard_map/ppermute | solution.py:9
  76.8 1.2 collective-permute-start.4
  78.1 54.8 %collective-permute-done.3 = bf16[64,96]{1,0:T(8,128)(2,1)S(1)} collective-permute-done((bf16[64,96]{1,0:T(8,128)(2,1)S(1)}, bf16[64,96]{1,0:T(8,128)(2,1)S(1)}, u32[]{:S(2)}, u32[]{:S(2)}) %collective-permute-start.3) | collective-permute-done | bytes 12320 | tf_op jit(solution)/shard_map/ppermute | solution.py:9
  132.9 1.2 collective-permute-start.5
  134.1 0.0 collective-permute-done.1
  134.1 1.3 collective-permute-done.2
  135.4 2.7 %convert_bitcast_fusion = (f32[8,8,96,128]{3,1,2,0:T(8,128)S(1)}, bf16[1,64,12288]{2,1,0:T(8,128)(2,1)S(1)}) fusion(s32[]{:T(128)S(6)} %select_n.40, bf16[1,64,12288]{2,1,0:T(8,128)(2,1)} %bitcast.3, bf16[1,64,12288]{2,1,0:T(8,128)(2,1)S(1)} %bitcast.43, bf16[1,64,12288]{2,1,0:T(8,128)(2,1)S(1)} %bitcast.42, bf16[1,64,12288]{2,1,0:T(8,128)(2,1)} %bitcast.41), kind=kLoop, calls=%fused_computation.12 | loop fusion | flops 3145728 | bytes 11010052
  138.1 0.4 collective-permute-start.6
  138.5 29.4 %constant_dynamic-slice_fusion = (bf16[256,1,1,12288]{3,1,2,0:T(2,128)(2,1)S(1)}, bf16[256,1,1,12288]{3,1,2,0:T(2,128)(2,1)}) fusion(bf16[256,2,1,12288]{3,1,2,0:T(2,128)(2,1)} %param.5, s32[]{:T(128)S(6)} %select_n.46, s32[]{:T(128)S(6)} %select_n.44), kind=kLoop, calls=%fused_computation.27 | loop fusion | bytes 25165832 | tf_op jit(solution)/shard_map/while/body/eval_jaxpr/jit(dynamic_index_in_dim)/dynamic_slice | solution.py:49
  167.9 0.0 collective-permute-done.4
  167.9 0.0 collective-permute-done.5
  168.0 2.1 collective-permute-start.7
  170.1 0.6 copy.14
  170.7 1.4 fusion.3
  172.0 11.6 %fusion.1 = f32[64,256]{1,0:T(8,128)S(1)} fusion(bf16[256,1,1,12288]{3,1,2,0:T(2,128)(2,1)} %get-tuple-element.30, bf16[8,8,96,128]{3,2,1,0:T(8,128)(2,1)S(1)} %bitcast.40), kind=kOutput, calls=%fused_computation.7 | convolution fusion | flops 402653184 | bytes 7929856 | tf_op jit(solution)/shard_map/dot_general | solution.py:52
  183.7 24.4 %collective-permute-done.7 = bf16[64,96]{1,0:T(8,128)(2,1)S(1)} collective-permute-done((bf16[64,96]{1,0:T(8,128)(2,1)S(1)}, bf16[64,96]{1,0:T(8,128)(2,1)S(1)}, u32[]{:S(2)}, u32[]{:S(2)}) %collective-permute-start.7) | collective-permute-done | bytes 12320 | tf_op jit(solution)/shard_map/while/body/eval_jaxpr/ppermute | solution.py:9
  208.1 0.0 collective-permute-done.6
  208.1 0.9 mul.33
  208.9 9.2 %fusion.10 = f32[64,256]{1,0:T(8,128)} fusion(f32[64,256]{1,0:T(8,128)S(1)} %fusion.1, bf16[256,1,1,12288]{3,1,2,0:T(2,128)(2,1)S(1)} %get-tuple-element.28, f32[8,8,96,128]{3,2,1,0:T(8,128)S(1)} %bitcast.39, bf16[64,12288]{1,0:T(8,128)(2,1)S(1)} %collective-permute-done.6), kind=kOutput, calls=%fused_computation.18 | convolution fusion | flops 405028864 | bytes 11141120 | tf_op jit(solution)/shard_map/while/body/eval_jaxpr/dot_general | solution.py:52
  218.1 0.0 all-reduce.2.cloned.1.call-update
  218.1 30.5 %all-reduce.2.cloned.1.call-done = f32[64,256]{1,0:T(8,128)} async-done(((f32[64,256]{1,0:T(8,128)}), f32[64,256]{1,0:T(8,128)}) %all-reduce.2.cloned.1.call-update) | async-done | bytes 65552 | tf_op jit(solution)/shard_map/psum | solution.py:66
  248.7 1.5 copy.32
  (1 shorter events, 0.0 us)
Async XLA Ops:
  6.5 23.7 %all-gather.2.cloned.1.call-start = ((), (), s32[]{:S(2)}) async-start(), calls=%async_computation | async-start | bytes 1966080 | tf_op jit(solution)/shard_map/all_gather | solution.py:21
  7.3 241.4 %all-reduce.2.cloned.1.call-start = ((), (), s32[]{:S(2)}) async-start(), calls=%async_computation.1 | async-start | bytes 131072 | tf_op jit(solution)/shard_map/psum | solution.py:66
  30.2 35.9 %collective-permute-start = (bf16[64,12288]{1,0:T(8,128)(2,1)}, bf16[64,12288]{1,0:T(8,128)(2,1)S(1)}, u32[]{:S(2)}, u32[]{:S(2)}) collective-permute-start(bf16[64,12288]{1,0:T(8,128)(2,1)} %all-gather.2.cloned.1.call-done), channel_id=1, source_target_pairs={{0,4},{4,8},{8,12},{12,16},{16,20},{20,24},{24,28},{28,0},{1,5},{5... | collective-permute-start | bytes 4718600 | tf_op jit(solution)/shard_map/ppermute | solution.py:9
  31.4 102.7 %collective-permute-start.1 = (bf16[64,12288]{1,0:T(8,128)(2,1)}, bf16[64,12288]{1,0:T(8,128)(2,1)S(1)}, u32[]{:S(2)}, u32[]{:S(2)}) collective-permute-start(bf16[64,12288]{1,0:T(8,128)(2,1)} %all-gather.2.cloned.1.call-done), channel_id=1, source_target_pairs={{0,8},{4,12},{8,16},{12,20},{16,24},{20,28},{24,0},{28,4},{1,9},{5... | collective-permute-start | bytes 4718600 | tf_op jit(solution)/shard_map/ppermute | solution.py:9
  66.1 69.3 %collective-permute-start.2 = (bf16[64,12288]{1,0:T(8,128)(2,1)S(1)}, bf16[64,12288]{1,0:T(8,128)(2,1)}, u32[]{:S(2)}, u32[]{:S(2)}) collective-permute-start(bf16[64,12288]{1,0:T(8,128)(2,1)S(1)} %collective-permute-done), channel_id=1, source_target_pairs={{0,8},{4,12},{8,16},{12,20},{16,24},{20,28},{24,0},{28,4},{1,9},{5... | collective-permute-start | bytes 4718600 | tf_op jit(solution)/shard_map/ppermute | solution.py:9
  74.0 58.9 %collective-permute-start.3 = (bf16[64,96]{1,0:T(8,128)(2,1)S(1)}, bf16[64,96]{1,0:T(8,128)(2,1)S(1)}, u32[]{:S(2)}, u32[]{:S(2)}) collective-permute-start(bf16[64,96]{1,0:T(8,128)(2,1)S(1)} %copy.7), channel_id=1, source_target_pairs={{0,4},{4,8},{8,12},{12,16},{16,20},{20,24},{24,28},{28,0},{1,5},{5... | collective-permute-start | bytes 36872 | tf_op jit(solution)/shard_map/ppermute | solution.py:9
  76.8 91.1 %collective-permute-start.4 = (bf16[64,96]{1,0:T(8,128)(2,1)S(1)}, bf16[64,96]{1,0:T(8,128)(2,1)S(1)}, u32[]{:S(2)}, u32[]{:S(2)}) collective-permute-start(bf16[64,96]{1,0:T(8,128)(2,1)S(1)} %copy.7), channel_id=1, source_target_pairs={{0,8},{4,12},{8,16},{12,20},{16,24},{20,28},{24,0},{28,4},{1,9},{5... | collective-permute-start | bytes 36872 | tf_op jit(solution)/shard_map/ppermute | solution.py:9
  132.9 35.0 %collective-permute-start.5 = (bf16[64,96]{1,0:T(8,128)(2,1)S(1)}, bf16[64,96]{1,0:T(8,128)(2,1)S(1)}, u32[]{:S(2)}, u32[]{:S(2)}) collective-permute-start(bf16[64,96]{1,0:T(8,128)(2,1)S(1)} %collective-permute-done.3), channel_id=1, source_target_pairs={{0,8},{4,12},{8,16},{12,20},{16,24},{20,28},{24,0},{28,4},{1,9},{5... | collective-permute-start | bytes 36872 | tf_op jit(solution)/shard_map/ppermute | solution.py:9
  138.1 69.9 %collective-permute-start.6 = (bf16[64,12288]{1,0:T(8,128)(2,1)S(1)}, bf16[64,12288]{1,0:T(8,128)(2,1)S(1)}, u32[]{:S(2)}, u32[]{:S(2)}) collective-permute-start(bf16[64,12288]{1,0:T(8,128)(2,1)S(1)} %bitcast.44), channel_id=1, source_target_pairs={{0,16},{4,20},{8,24},{12,28},{16,0},{20,4},{24,8},{28,12},{1,17},{... | collective-permute-start | bytes 4718600 | tf_op jit(solution)/shard_map/while/body/eval_jaxpr/ppermute | solution.py:9
  168.0 40.1 %collective-permute-start.7 = (bf16[64,96]{1,0:T(8,128)(2,1)S(1)}, bf16[64,96]{1,0:T(8,128)(2,1)S(1)}, u32[]{:S(2)}, u32[]{:S(2)}) collective-permute-start(bf16[64,96]{1,0:T(8,128)(2,1)S(1)} %get-tuple-element.18), channel_id=1, source_target_pairs={{0,16},{4,20},{8,24},{12,28},{16,0},{20,4},{24,8},{28,12},{1,17},{... | collective-permute-start | bytes 36872 | tf_op jit(solution)/shard_map/while/body/eval_jaxpr/ppermute | solution.py:9
Sparse Core Ops, SparseCore 0:
  8.9 21.2 all-gather.1
  218.3 30.3 all-reduce.1
where the time goes:
time: 260 us; the launch traced here: 257 us
  waiting for transfers between devices  168 us (65%)
  local copies, waits for them, and re-layouts  32.4 us (12%)
  matrix products  20.8 us (8%)
  between operations  13.5 us (5%)
  starting transfers between devices  11.4 us (4%)
  blocking collectives  6.57 us (3%)
  other arithmetic  4.1 us (2%)
    ppermute x8, waiting for transfers between devices, passed_along(): return lax.ppermute(x, axis, [(i, (i + by) % size) for i in range(size)])  114 us
    psum x1, waiting for transfers between devices, per_device(): product = lax.psum(running, 'team')  30.5 us
    dynamic_slice x1, local copies, waits for them, and re-layouts, contribute(): lax.dynamic_index_in_dim(cov_local, jnp.mod(stop_num, cycle_stops), 1, ke...  29.4 us
    all_gather x1, waiting for transfers between devices, per_device(): lax.all_gather(loadings, 'team', axis=1, tiled=True)  22.9 us
    dot_general x2, matrix products, contribute(): lax.dot_general(scaled, cov_slab, (((1,), (1,)), ((), ())), preferred_ele...  20.8 us
    ppermute x8, starting transfers between devices, passed_along(): return lax.ppermute(x, axis, [(i, (i + by) % size) for i in range(size)])  11.3 us
    all_gather x1, blocking collectives, per_device(): lax.all_gather(scales, 'team', axis=1, tiled=True)  6.57 us
  transfers between devices with their start and end apart: 10, of which 6 were waited for; matrix products, arithmetic and copies ran while one was open for 18% of the time, Pallas kernels for 0%

commit v1 on v0

v1 whole, which is shorter than its diff:
```python
import functools

import jax
import jax.numpy as jnp
from jax import lax
from jax.experimental import pallas as pl
from jax.experimental.pallas import tpu as pltpu
from jax.sharding import PartitionSpec as P

LANES = 128


def remote(src, dst, send_sem, recv_sem, blk, team):
    return pltpu.make_async_remote_copy(
        src_ref=src,
        dst_ref=dst,
        send_sem=send_sem,
        recv_sem=recv_sem,
        device_id={"blk": blk, "team": team},
        device_id_type=pl.DeviceIdType.MESH,
    )


def kernel(
    n_blk,
    n_team,
    load_ref,
    scale_ref,
    cov_ref,
    out_ref,
    cov_buf,
    own,
    held,
    total,
    parts,
    cov_sem,
    hub_sem,
    recv_sem,
    up_sem,
    down_sem,
    side_sem,
    sum_send,
    sum_recv,
):
    n_rows, _, stops, _ = cov_ref.shape
    pieces, n_loads, width = own.shape
    depth = width // LANES
    count = n_team * pieces
    length = n_blk // 2
    blk, team = lax.axis_index("blk"), lax.axis_index("team")
    place = blk // 2
    side = blk + 1 - 2 * (blk % 2)
    relays = (blk % 2) == (team % 2)
    own_stop, own_team = blk // n_team, blk % n_team

    barrier = pltpu.get_barrier_semaphore()

    def greet(b, t):
        pl.semaphore_signal(
            barrier, inc=1, device_id={"blk": b, "team": t}, device_id_type=pl.DeviceIdType.MESH
        )

    for away in range(1, n_team):
        greet(blk, (team + away) % n_team)
    greet(side, team)

    @pl.when(relays & (place > 0))
    def _():
        greet(blk - 2, team)

    @pl.when(relays & (place < length - 1))
    def _():
        greet(blk + 2, team)

    scale = scale_ref[...].astype(jnp.float32).T
    for h in range(pieces):
        cols = []
        for n in range(depth):
            g = h * depth + n
            x = load_ref[:, g * LANES : (g + 1) * LANES].astype(jnp.float32)
            cols.append((x * scale[:, g : g + 1]).astype(jnp.bfloat16))
        own[h] = jnp.concatenate(cols, axis=1) if depth > 1 else cols[0]

    def order(k):
        pair = (team // 2) * 2
        late = jnp.maximum(k - 2 * pieces, 0)
        m_near = pair + (team % 2 + k // pieces) % 2
        m_far = (pair + 2 + late % (n_team - 2)) % n_team
        near = k < 2 * pieces
        m = jnp.where(near, m_near, m_far)
        h = jnp.where(near, k % pieces, late // (n_team - 2))
        return m, m * pieces + h

    ends = jnp.where(place > 0, 1, 0) + jnp.where(place < length - 1, 1, 0)
    pl.semaphore_wait(barrier, n_team + jnp.where(relays, ends, 0))

    def to_hub(h):
        at = team * pieces + h
        return remote(
            own.at[h], held.at[own_stop, at], hub_sem.at[h], recv_sem.at[own_stop, at], blk, own_team
        )

    @pl.when(team != own_team)
    def _():
        for h in range(pieces):
            to_hub(h).start()

    @pl.when(team == own_team)
    def _():
        for h in range(pieces):
            held[own_stop, team * pieces + h] = own[h]

    @pl.loop(0, count)
    def _(k):
        _, at = order(k)

        @pl.loop(0, depth)
        def _(n):
            j = at * depth + n
            pltpu.make_async_copy(cov_ref.at[:, j], cov_buf.at[j], cov_sem.at[at]).start()

    flat = cov_buf.reshape(count * depth, n_rows * stops, LANES)
    total[...] = jnp.zeros_like(total)
    row_stop = lax.broadcasted_iota(jnp.int32, (n_rows * stops, n_loads), 0) % stops

    def where_is(stop):
        block = n_team * stop + team
        home = block // 2
        apart = jnp.where(home > place, home - place, place - home)
        goes_up = relays & (home <= place) & (place < length - 1)
        goes_down = relays & (place <= home) & (place > 0)
        return block, apart, goes_up, goes_down

    def onward(stop, at, sems, b):
        piece = held.at[stop, at]
        return remote(piece, piece, sems.at[stop, at], recv_sem.at[stop, at], b, team)

    @pl.loop(0, count + length - 1)
    def _(step):
        @pl.when(step < count)
        def _():
            _, at = order(step)
            loaded = cov_buf.at[pl.ds(at * depth, depth)]
            pltpu.make_async_copy(loaded, loaded, cov_sem.at[at]).wait()

        @pl.loop(0, stops)
        def _(stop):
            block, apart, goes_up, goes_down = where_is(stop)
            k = step - apart

            @pl.when((k >= 0) & (k < count))
            def _():
                m, at = order(k)

                @pl.when((block != blk) | (m != team))
                def _():
                    onward(stop, at, side_sem, side).wait_recv()

                @pl.when(goes_up)
                def _():
                    onward(stop, at, up_sem, blk + 2).start()

                @pl.when(goes_down)
                def _():
                    onward(stop, at, down_sem, blk - 2).start()

                @pl.when(relays)
                def _():
                    onward(stop, at, side_sem, side).start()

                cov = [flat[at * depth + n] for n in range(depth)]
                cov = jnp.concatenate(cov, axis=1) if depth > 1 else cov[0]
                term = lax.dot_general(
                    cov, held[stop, at], (((1,), (1,)), ((), ())), preferred_element_type=jnp.float32
                )
                total[:, 0:n_loads] += jnp.where(row_stop == stop, term, 0.0)

    part = total[pl.ds(0, n_rows, stride=stops), :]
    for stop in range(1, stops):
        part = part + total[pl.ds(stop, n_rows, stride=stops), :]
    parts[team] = part.T[0:n_loads, :]

    def exchange(away):
        return remote(
            parts.at[team],
            parts.at[team],
            sum_send.at[away],
            sum_recv.at[team],
            blk,
            (team + away) % n_team,
        )

    def arrival(m):
        return remote(parts.at[m], parts.at[m], sum_send.at[0], sum_recv.at[m], blk, m)

    for away in range(1, n_team):
        exchange(away).start()

    @pl.when(team != own_team)
    def _():
        for h in range(pieces):
            to_hub(h).wait_send()

    @pl.loop(0, stops)
    def _(stop):
        _, _, goes_up, goes_down = where_is(stop)

        @pl.loop(0, count)
        def _(at):
            @pl.when(goes_up)
            def _():
                onward(stop, at, up_sem, blk + 2).wait_send()

            @pl.when(goes_down)
            def _():
                onward(stop, at, down_sem, blk - 2).wait_send()

            @pl.when(relays)
            def _():
                onward(stop, at, side_sem, side).wait_send()

    for away in range(1, n_team):
        exchange(away).wait_send()
        arrival((team + away) % n_team).wait_recv()
    result = parts[0]
    for m in range(1, n_team):
        result = result + parts[m]
    out_ref[...] = result


def per_device(n_blk, n_team, loadings, scales, cov):
    n_loads, n_cols = loadings.shape
    n_rows, stops, _, block = cov.shape
    tiles = n_cols // LANES
    pieces = 3 if tiles % 3 == 0 else 1
    width = n_cols // pieces
    count = n_team * pieces
    by_tile = cov[:, :, 0, :].reshape(n_rows, stops, block // LANES, LANES).transpose(0, 2, 1, 3)
    dma = pltpu.SemaphoreType.DMA
    return pl.pallas_call(
        functools.partial(kernel, n_blk, n_team),
        out_shape=jax.ShapeDtypeStruct((n_loads, n_rows), jnp.float32),
        in_specs=[
            pl.BlockSpec(memory_space=pltpu.VMEM),
            pl.BlockSpec(memory_space=pltpu.VMEM),
            pl.BlockSpec(memory_space=pl.ANY),
        ],
        out_specs=pl.BlockSpec(memory_space=pltpu.VMEM),
        scratch_shapes=[
            pltpu.VMEM((block // LANES, n_rows, stops, LANES), jnp.bfloat16),
            pltpu.VMEM((pieces, n_loads, width), jnp.bfloat16),
            pltpu.VMEM((stops, count, n_loads, width), jnp.bfloat16),
            pltpu.VMEM((n_rows * stops, LANES), jnp.float32),
            pltpu.VMEM((n_team, n_loads, n_rows), jnp.float32),
            dma((count,)),
            dma((pieces,)),
            dma((stops, count)),
            dma((stops, count)),
            dma((stops, count)),
            dma((stops, count)),
            dma((n_team,)),
            dma((n_team,)),
        ],
        compiler_params=pltpu.CompilerParams(
            collective_id=0, has_side_effects=True, vmem_limit_bytes=44 << 20
        ),
    )(loadings, scales.T, by_tile)


def solution(mesh):
    placed = (P(None, ("blk", "team")), P(None, ("blk", "team")), P("blk", None, "team", None))
    return jax.shard_map(
        functools.partial(per_device, mesh.shape["blk"], mesh.shape["team"]),
        mesh=mesh,
        in_specs=placed,
        out_specs=P(None, "blk"),
        check_vma=False,
    )
```

time: 260 us -> 64.3 us (0.25); the launches traced: 257 us -> 64.1 us
  waiting for transfers between devices: 168 us -> 0 us
  Pallas kernels: 0 us -> 61.8 us
  local copies, waits for them, and re-layouts: 32.4 us -> 2.32 us
  matrix products: 20.8 us -> 0 us
  between operations: 13.5 us -> 0.01 us
  starting transfers between devices: 11.4 us -> 0 us
  blocking collectives: 6.57 us -> 0 us
  other arithmetic: 4.1 us -> 0 us
    ppermute x8 -> x0, waiting for transfers between devices: 114 us -> none  [passed_along(): return lax.ppermute(x, axis, [(i, (i + by) % size) for i in range(size)])]
    pallas_call x0 -> x1, Pallas kernels: none -> 61.8 us  [per_device(): pl.pallas_call(functools.partial(kernel, n_blk, n_team), out_shape=jax.Sh...]
    psum x1 -> x0, waiting for transfers between devices: 30.5 us -> none  [per_device(): product = lax.psum(running, 'team')]
    dynamic_slice x1 -> x0, local copies, waits for them, and re-layouts: 29.4 us -> none  [contribute(): lax.dynamic_index_in_dim(cov_local, jnp.mod(stop_num, cycle_stops), 1, ke...]
    all_gather x1 -> x0, waiting for transfers between devices: 22.9 us -> none  [per_device(): lax.all_gather(loadings, 'team', axis=1, tiled=True)]
    dot_general x2 -> x0, matrix products: 20.8 us -> none  [contribute(): lax.dot_general(scaled, cov_slab, (((1,), (1,)), ((), ())), preferred_ele...]
    ppermute x8 -> x0, starting transfers between devices: 11.3 us -> none  [passed_along(): return lax.ppermute(x, axis, [(i, (i + by) % size) for i in range(size)])]
    all_gather x1 -> x0, blocking collectives: 6.57 us -> none  [per_device(): lax.all_gather(scales, 'team', axis=1, tiled=True)]
  transfers between devices with their start and end apart: 10 -> 0, of which waited for: 6 -> 0; matrix products, arithmetic and copies ran while one was open for 18% -> 0% of each run, Pallas kernels for 0% -> 0%
where the time goes in v1:
time: 64.3 us; the launch traced here: 64.1 us
  Pallas kernels  61.8 us (96%)
  local copies, waits for them, and re-layouts  2.32 us (4%)
    pallas_call x1, Pallas kernels, per_device(): pl.pallas_call(functools.partial(kernel, n_blk, n_team), out_shape=jax.Sh...  61.8 us
    unnamed x5, local copies, waits for them, and re-layouts  2.32 us

profile of v1, /device:TPU:5, one launch (start us, length us, event | category | flops | bytes accessed | tf_op | source)
XLA Modules:
  0.0 64.1 jit_solution(4904600996363213396)
XLA Ops:
  0.0 0.0 copy-start
  0.0 1.0 %copy-done = bf16[64,3072]{1,0:T(8,128)(2,1)S(1)} copy-done((bf16[64,3072]{1,0:T(8,128)(2,1)S(1)}, bf16[64,3072]{1,0:T(8,128)(2,1)}, u32[]{:S(2)}) %copy-start) | copy-done | bytes 393240
  1.0 0.0 copy-start.1
  1.0 0.7 %copy-done.1 = bf16[64,24]{0,1:T(8,128)(2,1)S(1)} copy-done((bf16[64,24]{0,1:T(8,128)(2,1)S(1)}, bf16[64,24]{0,1:T(8,128)(2,1)}, u32[]{:S(2)}) %copy-start.1) | copy-done | bytes 3096
  1.7 61.8 %shard_map.37 = f32[64,256]{1,0:T(8,128)S(1)} custom-call(bf16[64,3072]{1,0:T(8,128)(2,1)S(1)} %copy-done, bf16[24,64]{1,0:T(8,128)(2,1)S(1)} %bitcast.4, bf16[256,96,2,128]{3,2,1,0:T(2,128)(2,1)} %bitcast.5), custom_call_target="tpu_custom_call" | custom-call | tf_op jit(solution)/shard_map/pallas_call | solution.py:240
  63.5 0.6 copy.5
Async XLA Ops:
  0.0 1.0 %copy-start = (bf16[64,3072]{1,0:T(8,128)(2,1)S(1)}, bf16[64,3072]{1,0:T(8,128)(2,1)}, u32[]{:S(2)}) copy-start(bf16[64,3072]{1,0:T(8,128)(2,1)} %load_ref.1) | copy-start | bytes 1179652
  1.0 0.7 %copy-start.1 = (bf16[64,24]{0,1:T(8,128)(2,1)S(1)}, bf16[64,24]{0,1:T(8,128)(2,1)}, u32[]{:S(2)}) copy-start(bf16[64,24]{0,1:T(8,128)(2,1)} %param.4) | copy-start | bytes 9220

commit v2 on v1

--- a/solution.py
+++ b/solution.py
@@ -8,6 +8,7 @@
 from jax.sharding import PartitionSpec as P
 
 LANES = 128
+AHEAD = 4
 
 
 def remote(src, dst, send_sem, recv_sem, blk, team):
@@ -24,15 +25,18 @@
 def kernel(
     n_blk,
     n_team,
+    load_hbm,
+    scale_hbm,
+    cov_ref,
+    out_ref,
     load_ref,
     scale_ref,
-    cov_ref,
-    out_ref,
     cov_buf,
     own,
     held,
     total,
     parts,
+    load_sem,
     cov_sem,
     hub_sem,
     recv_sem,
@@ -72,14 +76,10 @@
     def _():
         greet(blk + 2, team)
 
-    scale = scale_ref[...].astype(jnp.float32).T
-    for h in range(pieces):
-        cols = []
-        for n in range(depth):
-            g = h * depth + n
-            x = load_ref[:, g * LANES : (g + 1) * LANES].astype(jnp.float32)
-            cols.append((x * scale[:, g : g + 1]).astype(jnp.bfloat16))
-        own[h] = jnp.concatenate(cols, axis=1) if depth > 1 else cols[0]
+    loads = pltpu.make_async_copy(load_hbm, load_ref, load_sem.at[0])
+    scales = pltpu.make_async_copy(scale_hbm, scale_ref, load_sem.at[1])
+    scales.start()
+    loads.start()
 
     def order(k):
         pair = (team // 2) * 2
@@ -91,6 +91,28 @@
         h = jnp.where(near, k % pieces, late // (n_team - 2))
         return m, m * pieces + h
 
+    def fetch(k):
+        _, at = order(k)
+
+        @pl.loop(0, depth)
+        def _(n):
+            j = at * depth + n
+            pltpu.make_async_copy(cov_ref.at[:, j], cov_buf.at[j], cov_sem.at[at]).start()
+
+    for k in range(min(AHEAD, count)):
+        fetch(k)
+
+    scales.wait()
+    loads.wait()
+    scale = scale_ref[...].astype(jnp.float32).T
+    for h in range(pieces):
+        cols = []
+        for n in range(depth):
+            g = h * depth + n
+            x = load_ref[:, g * LANES : (g + 1) * LANES].astype(jnp.float32)
+            cols.append((x * scale[:, g : g + 1]).astype(jnp.bfloat16))
+        own[h] = jnp.concatenate(cols, axis=1) if depth > 1 else cols[0]
+
     ends = jnp.where(place > 0, 1, 0) + jnp.where(place < length - 1, 1, 0)
     pl.semaphore_wait(barrier, n_team + jnp.where(relays, ends, 0))
 
@@ -110,18 +132,15 @@
         for h in range(pieces):
             held[own_stop, team * pieces + h] = own[h]
 
-    @pl.loop(0, count)
-    def _(k):
-        _, at = order(k)
-
-        @pl.loop(0, depth)
-        def _(n):
-            j = at * depth + n
-            pltpu.make_async_copy(cov_ref.at[:, j], cov_buf.at[j], cov_sem.at[at]).start()
-
     flat = cov_buf.reshape(count * depth, n_rows * stops, LANES)
     total[...] = jnp.zeros_like(total)
-    row_stop = lax.broadcasted_iota(jnp.int32, (n_rows * stops, n_loads), 0) % stops
+    row_stop = lax.broadcasted_iota(jnp.int32, total.shape, 0) % stops
+    col_stop = lax.broadcasted_iota(jnp.int32, total.shape, 1) // n_loads
+    first, last = team // 2, (n_team // 2) * (stops - 1) + team // 2
+    lag = jnp.maximum(
+        jnp.where(first > place, first - place, place - first),
+        jnp.where(last > place, last - place, place - last),
+    )
 
     def where_is(stop):
         block = n_team * stop + team
@@ -137,12 +156,6 @@
 
     @pl.loop(0, count + length - 1)
     def _(step):
-        @pl.when(step < count)
-        def _():
-            _, at = order(step)
-            loaded = cov_buf.at[pl.ds(at * depth, depth)]
-            pltpu.make_async_copy(loaded, loaded, cov_sem.at[at]).wait()
-
         @pl.loop(0, stops)
         def _(stop):
             block, apart, goes_up, goes_down = where_is(stop)
@@ -168,17 +181,33 @@
                 def _():
                     onward(stop, at, side_sem, side).start()
 
-                cov = [flat[at * depth + n] for n in range(depth)]
-                cov = jnp.concatenate(cov, axis=1) if depth > 1 else cov[0]
+        @pl.when(step + AHEAD < count)
+        def _():
+            fetch(step + AHEAD)
+
+        ready = step - lag
+
+        @pl.when((ready >= 0) & (ready < count))
+        def _():
+            _, at = order(ready)
+            loaded = cov_buf.at[pl.ds(at * depth, depth)]
+            pltpu.make_async_copy(loaded, loaded, cov_sem.at[at]).wait()
+            cov = [flat[at * depth + n] for n in range(depth)]
+            cov = jnp.concatenate(cov, axis=1) if depth > 1 else cov[0]
+
+            @pl.loop(0, stops // 2)
+            def _(pair):
+                scaled = jnp.concatenate([held[2 * pair, at], held[2 * pair + 1, at]], axis=0)
                 term = lax.dot_general(
-                    cov, held[stop, at], (((1,), (1,)), ((), ())), preferred_element_type=jnp.float32
+                    cov, scaled, (((1,), (1,)), ((), ())), preferred_element_type=jnp.float32
                 )
-                total[:, 0:n_loads] += jnp.where(row_stop == stop, term, 0.0)
+                total[...] += jnp.where(row_stop == col_stop + 2 * pair, term, 0.0)
 
     part = total[pl.ds(0, n_rows, stride=stops), :]
     for stop in range(1, stops):
         part = part + total[pl.ds(stop, n_rows, stride=stops), :]
-    parts[team] = part.T[0:n_loads, :]
+    part = part.T
+    parts[team] = part[0:n_loads, :] + part[n_loads : 2 * n_loads, :]
 
     def exchange(away):
         return remote(
@@ -232,7 +261,7 @@
     n_loads, n_cols = loadings.shape
     n_rows, stops, _, block = cov.shape
     tiles = n_cols // LANES
-    pieces = 3 if tiles % 3 == 0 else 1
+    pieces = max(p for p in (1, 3, 4) if tiles % p == 0)
     width = n_cols // pieces
     count = n_team * pieces
     by_tile = cov[:, :, 0, :].reshape(n_rows, stops, block // LANES, LANES).transpose(0, 2, 1, 3)
@@ -241,17 +270,20 @@
         functools.partial(kernel, n_blk, n_team),
         out_shape=jax.ShapeDtypeStruct((n_loads, n_rows), jnp.float32),
         in_specs=[
-            pl.BlockSpec(memory_space=pltpu.VMEM),
-            pl.BlockSpec(memory_space=pltpu.VMEM),
+            pl.BlockSpec(memory_space=pl.ANY),
+            pl.BlockSpec(memory_space=pl.ANY),
             pl.BlockSpec(memory_space=pl.ANY),
         ],
         out_specs=pl.BlockSpec(memory_space=pltpu.VMEM),
         scratch_shapes=[
+            pltpu.VMEM((n_loads, n_cols), jnp.bfloat16),
+            pltpu.VMEM((tiles, n_loads), jnp.bfloat16),
             pltpu.VMEM((block // LANES, n_rows, stops, LANES), jnp.bfloat16),
             pltpu.VMEM((pieces, n_loads, width), jnp.bfloat16),
             pltpu.VMEM((stops, count, n_loads, width), jnp.bfloat16),
-            pltpu.VMEM((n_rows * stops, LANES), jnp.float32),
+            pltpu.VMEM((n_rows * stops, 2 * n_loads), jnp.float32),
             pltpu.VMEM((n_team, n_loads, n_rows), jnp.float32),
+            dma((2,)),
             dma((count,)),
             dma((pieces,)),
             dma((stops, count)),
@@ -262,7 +294,7 @@
             dma((n_team,)),
         ],
         compiler_params=pltpu.CompilerParams(
-            collective_id=0, has_side_effects=True, vmem_limit_bytes=44 << 20
+            collective_id=0, has_side_effects=True, vmem_limit_bytes=56 << 20
         ),
     )(loadings, scales.T, by_tile)
 

time: 64.3 us -> 70.8 us (1.10)
  Pallas kernels: 61.8 us -> 69.1 us
  local copies, waits for them, and re-layouts: 2.32 us -> 1.47 us
    pallas_call x1, Pallas kernels: 61.8 us -> 69.1 us  [per_device(): pl.pallas_call(functools.partial(kernel, n_blk, n_team), out_shape=jax.Sh...]
    unnamed x5 -> x1, local copies, waits for them, and re-layouts: 2.32 us -> 1.47 us
where the time goes in v2:
time: 70.8 us; the launch traced here: 70.6 us
  Pallas kernels  69.1 us (98%)
  local copies, waits for them, and re-layouts  1.47 us (2%)
    pallas_call x1, Pallas kernels, per_device(): pl.pallas_call(functools.partial(kernel, n_blk, n_team), out_shape=jax.Sh...  69.1 us
    unnamed x1, local copies, waits for them, and re-layouts  1.47 us

profile of v2, /device:TPU:5, one launch (start us, length us, event | category | flops | bytes accessed | tf_op | source)
XLA Modules:
  0.0 70.6 jit_solution(8309795960700876664)
XLA Ops:
  0.0 69.1 %shard_map.37 = f32[64,256]{1,0:T(8,128)} custom-call(bf16[64,3072]{1,0:T(8,128)(2,1)} %load_hbm.1, bf16[24,64]{1,0:T(8,128)(2,1)} %bitcast.5, bf16[256,96,2,128]{3,2,1,0:T(2,128)(2,1)} %bitcast.4), custom_call_target="tpu_custom_call" | custom-call | tf_op jit(solution)/shard_map/pallas_call | solution.py:269
  69.1 1.5 %copy.5 = f32[64,256]{1,0:T(8,128)} copy(f32[64,256]{1,0:T(8,128)} %shard_map.37) | data formatting | bytes 131072

commit v3 on v2

--- a/solution.py
+++ b/solution.py
@@ -8,7 +8,6 @@
 from jax.sharding import PartitionSpec as P
 
 LANES = 128
-AHEAD = 4
 
 
 def remote(src, dst, send_sem, recv_sem, blk, team):
@@ -91,16 +90,11 @@
         h = jnp.where(near, k % pieces, late // (n_team - 2))
         return m, m * pieces + h
 
-    def fetch(k):
+    @pl.loop(0, count)
+    def _(k):
         _, at = order(k)
-
-        @pl.loop(0, depth)
-        def _(n):
-            j = at * depth + n
-            pltpu.make_async_copy(cov_ref.at[:, j], cov_buf.at[j], cov_sem.at[at]).start()
-
-    for k in range(min(AHEAD, count)):
-        fetch(k)
+        tiles = cov_ref.at[:, pl.ds(at * depth, depth)]
+        pltpu.make_async_copy(tiles, cov_buf.at[at], cov_sem.at[at]).start()
 
     scales.wait()
     loads.wait()
@@ -132,7 +126,6 @@
         for h in range(pieces):
             held[own_stop, team * pieces + h] = own[h]
 
-    flat = cov_buf.reshape(count * depth, n_rows * stops, LANES)
     total[...] = jnp.zeros_like(total)
     row_stop = lax.broadcasted_iota(jnp.int32, total.shape, 0) % stops
     col_stop = lax.broadcasted_iota(jnp.int32, total.shape, 1) // n_loads
@@ -181,18 +174,14 @@
                 def _():
                     onward(stop, at, side_sem, side).start()
 
-        @pl.when(step + AHEAD < count)
-        def _():
-            fetch(step + AHEAD)
-
         ready = step - lag
 
         @pl.when((ready >= 0) & (ready < count))
         def _():
             _, at = order(ready)
-            loaded = cov_buf.at[pl.ds(at * depth, depth)]
+            loaded = cov_buf.at[at]
             pltpu.make_async_copy(loaded, loaded, cov_sem.at[at]).wait()
-            cov = [flat[at * depth + n] for n in range(depth)]
+            cov = [cov_buf[at, :, n].reshape(n_rows * stops, LANES) for n in range(depth)]
             cov = jnp.concatenate(cov, axis=1) if depth > 1 else cov[0]
 
             @pl.loop(0, stops // 2)
@@ -261,7 +250,7 @@
     n_loads, n_cols = loadings.shape
     n_rows, stops, _, block = cov.shape
     tiles = n_cols // LANES
-    pieces = max(p for p in (1, 3, 4) if tiles % p == 0)
+    pieces = max(p for p in (1, 3) if tiles % p == 0)
     width = n_cols // pieces
     count = n_team * pieces
     by_tile = cov[:, :, 0, :].reshape(n_rows, stops, block // LANES, LANES).transpose(0, 2, 1, 3)
@@ -278,7 +267,7 @@
         scratch_shapes=[
             pltpu.VMEM((n_loads, n_cols), jnp.bfloat16),
             pltpu.VMEM((tiles, n_loads), jnp.bfloat16),
-            pltpu.VMEM((block // LANES, n_rows, stops, LANES), jnp.bfloat16),
+            pltpu.VMEM((count, n_rows, width // LANES, stops, LANES), jnp.bfloat16),
             pltpu.VMEM((pieces, n_loads, width), jnp.bfloat16),
             pltpu.VMEM((stops, count, n_loads, width), jnp.bfloat16),
             pltpu.VMEM((n_rows * stops, 2 * n_loads), jnp.float32),

time: 70.8 us -> 61.2 us (0.86)
  Pallas kernels: 69.1 us -> 59.6 us
    pallas_call x1, Pallas kernels: 69.1 us -> 59.6 us  [per_device(): pl.pallas_call(functools.partial(kernel, n_blk, n_team), out_shape=jax.Sh...]
where the time goes in v3:
time: 61.2 us; the launch traced here: 61 us
  Pallas kernels  59.6 us (97%)
  local copies, waits for them, and re-layouts  1.47 us (2%)
    pallas_call x1, Pallas kernels, per_device(): pl.pallas_call(functools.partial(kernel, n_blk, n_team), out_shape=jax.Sh...  59.6 us
    unnamed x1, local copies, waits for them, and re-layouts  1.47 us

profile of v3, /device:TPU:5, one launch (start us, length us, event | category | flops | bytes accessed | tf_op | source)
XLA Modules:
  0.0 61.0 jit_solution(9596961365092099024)
XLA Ops:
  0.0 59.6 %shard_map.37 = f32[64,256]{1,0:T(8,128)} custom-call(bf16[64,3072]{1,0:T(8,128)(2,1)} %load_hbm.1, bf16[24,64]{1,0:T(8,128)(2,1)} %bitcast.5, bf16[256,96,2,128]{3,2,1,0:T(2,128)(2,1)} %bitcast.4), custom_call_target="tpu_custom_call" | custom-call | tf_op jit(solution)/shard_map/pallas_call | solution.py:258
  59.6 1.5 %copy.5 = f32[64,256]{1,0:T(8,128)} copy(f32[64,256]{1,0:T(8,128)} %shard_map.37) | data formatting | bytes 131072
